TPU v7x, 512 devices: a whole 4x8x8 slice. The times are simulated.
512 devices in a mesh: grp: 16 (over y, z_lo), row: 32 (over z_hi, x, core).
Axes of the slice: x: 4, y: 8, z: 8 (z_hi: 4, z_lo: 2; z = z_hi * 2 + z_lo), core: 2. Of those that a mesh axis runs over, the one named last changes fastest.
Arguments:
- cov_prior: float32 [16384, 16384], P(('grp', 'row')), may hold values from -7 to 23, as said below
- courant_x_field: float32 [128, 128], replicated, may hold values from -0.35 to 0.35
- courant_y_field: float32 [128, 128], replicated, may hold values from -0.35 to 0.35
- obs_cells: int32 [2, 128], replicated, may hold values from 0 to 16383
- obs_var: float32 [2, 128], replicated, may hold values from 0.5 to 2
Outputs:
- analysis: float32 [16384, 16384], P('grp', 'row')
Inputs may be any that keep to these rules, and one draw needn't show every extreme that they name: `cov_prior`: symmetric and positive definite. `obs_cells`: a cell may be observed more than once in an update.
All inputs are finite; a program needn't handle non-finite values.
Results may differ from a plain program's by a relative error of at most 0.0002.
Values sent between devices are 32-bit elements; how exact they have to be, the bound alone decides.
A program may use at most 64 MiB of HBM per device.

v0:
```python
import jax
import jax.numpy as jnp
from jax import lax
from jax.sharding import PartitionSpec as P

ZONAL_POINTS = 128
NY = 128
NCELL = 16384
UPDATES = 2
diffusion = 0.1


def extended_2(block, sides, width):
    for axis, dim in sides:
        count = lax.axis_size(axis)
        forward = [(i, i + 1) for i in range(count - 1)]
        backward = [(target, source) for source, target in forward]
        low = lax.ppermute(
            lax.slice_in_dim(block, block.shape[dim] - width, None, axis=dim), axis, forward
        )
        high = lax.ppermute(lax.slice_in_dim(block, 0, width, axis=dim), axis, backward)
        block = jnp.concatenate([low, block, high], axis=dim)
    return block


def tendency_first(padded, u_part, v_part):
    middle = padded[:, 2:-2]
    center = middle[:, :, 2:-2]
    along_x = (
        8.0 * (middle[:, :, 3:-1] - middle[:, :, 1:-3]) - (middle[:, :, 4:] - middle[:, :, :-4])
    ) / 12.0
    column = padded[:, :, 2:-2]
    along_y = (8.0 * (column[:, 3:-1] - column[:, 1:-3]) - (column[:, 4:] - column[:, :-4])) / 12.0
    laplace = (
        middle[:, :, 3:-1] + middle[:, :, 1:-3] + column[:, 3:-1] + column[:, 1:-3] - 4.0 * center
    )
    return diffusion * laplace - u_part * along_x - v_part * along_y


def heun_whole(fields, courant_x_field, courant_y_field):
    slope_first = tendency_first(
        jnp.pad(fields, ((0, 0), (2, 2), (2, 2))), courant_x_field, courant_y_field
    )
    latter_increment = tendency_first(
        jnp.pad(fields + slope_first, ((0, 0), (2, 2), (2, 2))), courant_x_field, courant_y_field
    )
    return fields + 0.5 * (slope_first + latter_increment)


def tendency_last(extended, u_part, v_part):
    padded = jnp.pad(extended, ((0, 0), (2, 2), (0, 0)))
    middle = padded[2:-2]
    center = middle[:, 2:-2]
    along_x = (8.0 * (middle[:, 3:-1] - middle[:, 1:-3]) - (middle[:, 4:] - middle[:, :-4])) / 12.0
    column = padded[:, 2:-2]
    along_y = (8.0 * (column[3:-1] - column[1:-3]) - (column[4:] - column[:-4])) / 12.0
    laplace = middle[:, 3:-1] + middle[:, 1:-3] + column[3:-1] + column[1:-3] - 4.0 * center
    return diffusion * laplace - u_part * along_x - v_part * along_y


def linear_source_term(local_block, courant_x_field, courant_y_field):
    meridional_count = local_block.shape[0]
    first_row = lax.axis_index("grp") * meridional_count
    u_padded = jnp.pad(courant_x_field, ((4, 4), (0, 0)))
    v_padded = jnp.pad(courant_y_field, ((4, 4), (0, 0)))
    u_inner = lax.dynamic_slice_in_dim(u_padded, first_row + 4, meridional_count, 0)[:, :, None]
    v_inner = lax.dynamic_slice_in_dim(v_padded, first_row + 4, meridional_count, 0)[:, :, None]

    def section_slope(current):
        extended = extended_2(current, (("grp", 0),), 2)
        return tendency_last(extended, u_inner, v_inner)

    slope_first = section_slope(local_block)
    latter_increment = section_slope(local_block + slope_first)
    local_block = local_block + 0.5 * (slope_first + latter_increment)
    return local_block


def local(cov_prior, courant_x_field, courant_y_field, obs_cells, obs_var):
    row_count = cov_prior.shape[0]
    fields = cov_prior.reshape(row_count, NY, ZONAL_POINTS)
    fields = heun_whole(fields, courant_x_field, courant_y_field)
    advanced = fields.reshape(row_count, NCELL)
    members = lax.axis_size("row")
    zonal_extent = NCELL // members
    meridional_count = row_count * members // ZONAL_POINTS
    arrived_value = lax.all_to_all(advanced, "row", split_axis=1, concat_axis=0, tiled=True)
    predicted_tracer = linear_source_term(
        arrived_value.reshape(meridional_count, ZONAL_POINTS, zonal_extent),
        courant_x_field,
        courant_y_field,
    )
    posterior_mean = predicted_tracer.reshape(meridional_count * ZONAL_POINTS, zonal_extent)
    local_rows = posterior_mean.shape[0]
    first_cell = lax.axis_index("grp") * local_rows
    first_column = lax.axis_index("row") * zonal_extent
    for update_number in range(UPDATES):
        picked = obs_cells[update_number]
        row_offset = picked - first_cell
        row_owned = (row_offset >= 0) & (row_offset < local_rows)
        rows_part = jnp.where(
            row_owned[:, None], posterior_mean[jnp.clip(row_offset, 0, local_rows - 1)], 0.0
        )
        observed_rows = lax.psum(rows_part, "grp")
        column_offset = picked - first_column
        column_owned = (column_offset >= 0) & (column_offset < zonal_extent)
        safe_column = jnp.clip(column_offset, 0, zonal_extent - 1)
        cols_part = jnp.where(column_owned[None, :], posterior_mean[:, safe_column], 0.0)
        inner_part = jnp.where(column_owned[None, :], observed_rows[:, safe_column], 0.0)
        observed_cols, inner_block = lax.psum((cols_part, inner_part), "row")
        system = 0.5 * (inner_block + inner_block.T) + jnp.diag(obs_var[update_number])
        factor = jnp.linalg.cholesky(system)
        halfway = lax.linalg.triangular_solve(factor, observed_rows, left_side=True, lower=True)
        weights = lax.linalg.triangular_solve(
            factor, halfway, left_side=True, lower=True, transpose_a=True
        )
        posterior_mean = posterior_mean - jnp.dot(
            observed_cols, weights, precision=lax.Precision.HIGHEST
        )
    return posterior_mean


def solution(mesh):
    placed = (P(("grp", "row"), None), P(), P(), P(), P())
    return jax.shard_map(
        local, mesh=mesh, in_specs=placed, out_specs=P("grp", "row"), check_vma=False
    )
```

profile of v0, /device:TPU:8, one launch (start us, length us, event | category | flops | bytes accessed | tf_op | source)
XLA Modules:
  0.0 1064.2 jit_solution(17766533963469429662)
XLA Ops:
  6.5 2.0 copy.29
  8.6 2.6 bitcast_add_fusion.4
  11.2 4.0 fusion.20
  15.1 1.7 all_to_all.12
  16.9 1.2 copy.6
  18.1 54.5 %all_to_all.16 = f32[32,32,512]{2,0,1:T(8,128)S(1)} all-to-all(f32[32,32,512]{2,0,1:T(8,128)S(1)} %copy.6), channel_id=1, replica_groups=mesh['grp'=16,'row'=32] {'row'}, dimensions={1} | all-to-all | bytes 4194304 | tf_op jit(solution)/shard_map/all_to_all | solution.py:87
  72.5 1.1 fusion.66
  73.6 14.2 %collective-permute-start = (f32[2,128,512]{2,1,0:T(8,128)}, f32[2,128,512]{2,1,0:T(8,128)S(1)}, u32[]{:S(2)}, u32[]{:S(2)}) collective-permute-start(f32[2,128,512]{2,1,0:T(8,128)} %bitcast.2), channel_id=1, source_target_pairs={{0,32},{32,64},{64,96},{96,128},{128,160},{160,192},{192,224},{224... | collective-permute-start | bytes 1572872 | tf_op jit(solution)/shard_map/ppermute | solution.py:18
  87.8 1.9 collective-permute-start.1
  89.8 20.8 %collective-permute-done = f32[2,128,512]{2,1,0:T(8,128)S(1)} collective-permute-done((f32[2,128,512]{2,1,0:T(8,128)}, f32[2,128,512]{2,1,0:T(8,128)S(1)}, u32[]{:S(2)}, u32[]{:S(2)}) %collective-permute-start) | collective-permute-done | bytes 524320 | tf_op jit(solution)/shard_map/ppermute | solution.py:18
  110.6 0.5 collective-permute-done.1
  111.1 0.6 select_maximum_fusion.2
  111.7 1.8 fusion.62
  113.6 3.8 collective-permute-start.2
  117.4 3.0 collective-permute-start.3
  120.4 18.5 %collective-permute-done.2 = f32[2,128,512]{2,1,0:T(8,128)S(1)} collective-permute-done((f32[2,128,512]{2,1,0:T(8,128)S(1)}, f32[2,128,512]{2,1,0:T(8,128)S(1)}, u32[]{:S(2)}, u32[]{:S(2)}) %collective-permute-start.2) | collective-permute-done | bytes 524320 | tf_op jit(solution)/shard_map/ppermute | solution.py:18
  138.9 2.5 collective-permute-done.3
  141.5 0.6 select_maximum_fusion
  142.1 2.9 fusion.30
  145.0 2.6 gather_fusion.1
  147.6 0.8 broadcast_select_fusion.1
  148.5 1.8 copy.7
  150.3 2.6 gather_fusion
  153.0 0.9 select_bitcast_fusion.1
  153.9 131.3 %all-reduce.13.cloned.1.call-done = f32[128,512]{1,0:T(8,128)} async-done(((f32[128,512]{1,0:T(8,128)}), f32[128,512]{1,0:T(8,128)}) %all-reduce.13.cloned.1.call-update) | async-done | bytes 262160 | tf_op jit(solution)/shard_map/psum | solution.py:104
  285.3 1.1 copy.8
  286.4 0.6 gather_fusion.2
  287.1 0.7 select_bitcast_fusion.3
  287.8 0.2 all-reduce.15.cloned.1.call-start
  288.1 284.4 %all-reduce.19.cloned.1.call-done = (f32[1024,128]{0,1:T(8,128)}, f32[128,128]{0,1:T(8,128)}) async-done(((f32[1024,128]{0,1:T(8,128)}, f32[128,128]{0,1:T(8,128)}), (f32[1024,128]{0,1:T(8,128)}, f32[128,128]{0,1:T(8,128)})) %all-reduce.19.cloned.1.call-update) | async-done | bytes 589840 | tf_op jit(solution)/shard_map/psum | solution.py:110
  572.5 1.0 copy.10
  573.5 0.9 fusion.55
  574.4 0.1 copy.12
  574.5 0.1 copy.13
  574.6 11.7 %cholesky.44 = f32[128,128]{1,0:T(8,128)S(1)} custom-call(f32[128,128]{1,0:T(8,128)S(1)} %copy.13), custom_call_target="Cholesky" | custom-call | tf_op jit(solution)/shard_map/jit(cholesky)/cholesky | solution.py:112
  586.4 0.6 compare_reduce_fusion.1
  587.0 0.6 fusion.41
  587.6 9.8 custom-call.11
  597.4 0.4 fusion.49
  597.8 0.4 fusion.51
  598.2 3.4 convolution_subtract_fusion.1
  601.7 0.8 gather_fusion.4
  602.4 0.8 broadcast_select_fusion
  603.2 0.3 all-reduce.17.cloned.1.call-start
  603.5 1.8 copy.14
  605.3 2.6 gather_fusion.3
  608.0 0.9 select_bitcast_fusion
  608.9 132.8 %all-reduce.15.cloned.1.call-done = f32[128,512]{1,0:T(8,128)} async-done(((f32[128,512]{1,0:T(8,128)}), f32[128,512]{1,0:T(8,128)}) %all-reduce.15.cloned.1.call-update) | async-done | bytes 262160 | tf_op jit(solution)/shard_map/psum | solution.py:104
  741.6 1.1 copy.15
  742.8 0.6 gather_fusion.5
  743.5 0.6 select_bitcast_fusion.2
  744.2 0.1 copy.18
  744.3 284.4 %all-reduce.17.cloned.1.call-done = (f32[1024,128]{0,1:T(8,128)}, f32[128,128]{1,0:T(8,128)}) async-done(((f32[1024,128]{0,1:T(8,128)}, f32[128,128]{1,0:T(8,128)}), (f32[1024,128]{0,1:T(8,128)}, f32[128,128]{1,0:T(8,128)})) %all-reduce.17.cloned.1.call-update) | async-done | bytes 589840 | tf_op jit(solution)/shard_map/psum | solution.py:110
  1028.8 1.0 copy.17
  1029.8 0.9 fusion.48
  1030.6 0.1 copy.19
  1030.7 0.1 copy.20
  1030.8 11.7 %cholesky.55 = f32[128,128]{1,0:T(8,128)S(1)} custom-call(f32[128,128]{1,0:T(8,128)S(1)} %fusion.47), custom_call_target="Cholesky" | custom-call | tf_op jit(solution)/shard_map/jit(cholesky)/cholesky | solution.py:112
  1042.6 0.6 compare_reduce_fusion
  1043.2 0.7 fusion.42
  1043.9 9.8 custom-call.13
  1053.7 0.4 fusion.43
  1054.1 0.4 fusion.45
  1054.5 3.2 convolution_subtract_fusion
  (41 shorter events, 0.5 us)
Async XLA Ops:
  6.5 278.7 %all-reduce.13.cloned.1.call-start = ((), (), s32[]{:S(2)}) async-start(), calls=%async_computation.1 | async-start | bytes 524288 | tf_op jit(solution)/shard_map/psum | solution.py:104
  6.5 2.0 copy-start.5
  6.5 2.0 copy-start.6
  73.6 37.0 %collective-permute-start = (f32[2,128,512]{2,1,0:T(8,128)}, f32[2,128,512]{2,1,0:T(8,128)S(1)}, u32[]{:S(2)}, u32[]{:S(2)}) collective-permute-start(f32[2,128,512]{2,1,0:T(8,128)} %bitcast.2), channel_id=1, source_target_pairs={{0,32},{32,64},{64,96},{96,128},{128,160},{160,192},{192,224},{224... | collective-permute-start | bytes 1572872 | tf_op jit(solution)/shard_map/ppermute | solution.py:18
  87.8 23.3 %collective-permute-start.1 = (f32[2,128,512]{2,1,0:T(8,128)}, f32[2,128,512]{2,1,0:T(8,128)S(1)}, u32[]{:S(2)}, u32[]{:S(2)}) collective-permute-start(f32[2,128,512]{2,1,0:T(8,128)} %bitcast.4), channel_id=1, source_target_pairs={{32,0},{64,32},{96,64},{128,96},{160,128},{192,160},{224,192},{256... | collective-permute-start | bytes 1572872 | tf_op jit(solution)/shard_map/ppermute | solution.py:21
  113.5 6.8 copy-start.7
  113.6 25.3 %collective-permute-start.2 = (f32[2,128,512]{2,1,0:T(8,128)S(1)}, f32[2,128,512]{2,1,0:T(8,128)S(1)}, u32[]{:S(2)}, u32[]{:S(2)}) collective-permute-start(f32[2,128,512]{2,1,0:T(8,128)S(1)} %get-tuple-element.17), channel_id=1, source_target_pairs={{0,32},{32,64},{64,96},{96,128},{128,160},{160,192},{192,224},{224... | collective-permute-start | bytes 1572872 | tf_op jit(solution)/shard_map/ppermute | solution.py:18
  117.4 24.1 %collective-permute-start.3 = (f32[2,128,512]{2,1,0:T(8,128)S(1)}, f32[2,128,512]{2,1,0:T(8,128)S(1)}, u32[]{:S(2)}, u32[]{:S(2)}) collective-permute-start(f32[2,128,512]{2,1,0:T(8,128)S(1)} %get-tuple-element.16), channel_id=1, source_target_pairs={{32,0},{64,32},{96,64},{128,96},{160,128},{192,160},{224,192},{256... | collective-permute-start | bytes 1572872 | tf_op jit(solution)/shard_map/ppermute | solution.py:21
  145.0 3.5 copy-start
  148.4 424.1 %all-reduce.19.cloned.1.call-start = ((), (), s32[]{:S(2)}) async-start(), calls=%async_computation.4 | async-start | bytes 1179648 | tf_op jit(solution)/shard_map/psum | solution.py:110
  153.0 135.1 %copy-start.8 = (f32[2,128]{1,0:T(2,128)S(1)}, f32[2,128]{1,0:T(2,128)}, u32[]{:S(2)}) copy-start(f32[2,128]{1,0:T(2,128)} %param.14) | copy-start | bytes 3076
  285.3 312.1 %copy-start.2 = (f32[128,512]{1,0:T(8,128)S(1)}, f32[128,512]{1,0:T(8,128)}, u32[]{:S(2)}) copy-start(f32[128,512]{1,0:T(8,128)} %all-reduce.13.cloned.1.call-done) | copy-start | bytes 786436
  287.8 453.8 %all-reduce.15.cloned.1.call-start = ((), (), s32[]{:S(2)}) async-start(), calls=%async_computation.2 | async-start | bytes 524288 | tf_op jit(solution)/shard_map/psum | solution.py:104
  572.5 25.7 %copy-start.3 = (f32[1024,128]{0,1:T(8,128)S(1)}, f32[1024,128]{0,1:T(8,128)}, u32[]{:S(2)}) copy-start(f32[1024,128]{0,1:T(8,128)} %get-tuple-element.10) | copy-start | bytes 1572868
  603.2 425.5 %all-reduce.17.cloned.1.call-start = ((), (), s32[]{:S(2)}) async-start(), calls=%async_computation.3 | async-start | bytes 1179648 | tf_op jit(solution)/shard_map/psum | solution.py:110
  741.6 312.1 %copy-start.1 = (f32[128,512]{1,0:T(8,128)S(1)}, f32[128,512]{1,0:T(8,128)}, u32[]{:S(2)}) copy-start(f32[128,512]{1,0:T(8,128)} %all-reduce.15.cloned.1.call-done) | copy-start | bytes 786436
  1028.8 25.8 %copy-start.4 = (f32[1024,128]{0,1:T(8,128)S(1)}, f32[1024,128]{0,1:T(8,128)}, u32[]{:S(2)}) copy-start(f32[1024,128]{0,1:T(8,128)} %get-tuple-element.6) | copy-start | bytes 1572868
Sparse Core Ops, SparseCore 0:
  148.6 136.6 all-reduce.12
  288.5 283.9 all-reduce.18
  603.4 138.2 all-reduce.14
  744.8 283.9 all-reduce.16
where the time goes:
time: 1060 us
  waiting for transfers between devices  875 us (83%)
  other arithmetic  64.7 us (6%)
  blocking collectives  54.5 us (5%)
  local copies, waits for them, and re-layouts  24.5 us (2%)
  starting transfers between devices  23.4 us (2%)
  between operations  13.6 us (1%)
    psum x2, waiting for transfers between devices, local(): observed_cols, inner_block = lax.psum((cols_part, inner_part), 'row')  569 us
    psum x2, waiting for transfers between devices, local(): observed_rows = lax.psum(rows_part, 'grp')  264 us
    all_to_all x1, blocking collectives, local(): lax.all_to_all(advanced, 'row', split_axis=1, concat_axis=0, tiled=True)  54.5 us
    ppermute x2, waiting for transfers between devices, extended_2(): lax.ppermute(lax.slice_in_dim(block, block.shape[dim] - width, None, axis...  39.3 us
    another operation x7, other arithmetic, local(): factor = jnp.linalg.cholesky(system)  24.8 us
  transfers between devices with their start and end apart: 8, of which 8 were waited for; matrix products, arithmetic and copies ran while one was open for 1% of the time, Pallas kernels for 0%

commit v1 on v0

--- a/solution.py
+++ b/solution.py
@@ -101,7 +101,7 @@
         rows_part = jnp.where(
             row_owned[:, None], posterior_mean[jnp.clip(row_offset, 0, local_rows - 1)], 0.0
         )
-        observed_rows = lax.psum(rows_part, "grp")
+        observed_rows = jnp.sum(lax.all_gather(rows_part, "grp"), axis=0)
         column_offset = picked - first_column
         column_owned = (column_offset >= 0) & (column_offset < zonal_extent)
         safe_column = jnp.clip(column_offset, 0, zonal_extent - 1)

time: 1060 us -> 991 us (0.935)
  waiting for transfers between devices: 875 us -> 799 us
    psum x2 -> x0, waiting for transfers between devices: 264 us -> none  [local(): observed_rows = lax.psum(rows_part, 'grp')]
    all_gather x0 -> x2, waiting for transfers between devices: none -> 190 us  [local(): observed_rows = jnp.sum(lax.all_gather(rows_part, 'grp'), axis=0)]
where the time goes in v1:
time: 991 us
  waiting for transfers between devices  799 us (81%)
  other arithmetic  70.1 us (7%)
  blocking collectives  54.5 us (5%)
  starting transfers between devices  23.4 us (2%)
  local copies, waits for them, and re-layouts  22.5 us (2%)
  between operations  13.6 us (1%)
    psum x2, waiting for transfers between devices, local(): observed_cols, inner_block = lax.psum((cols_part, inner_part), 'row')  567 us
    all_gather x2, waiting for transfers between devices, local(): observed_rows = jnp.sum(lax.all_gather(rows_part, 'grp'), axis=0)  190 us
    all_to_all x1, blocking collectives, local(): lax.all_to_all(advanced, 'row', split_axis=1, concat_axis=0, tiled=True)  54.5 us
    ppermute x2, waiting for transfers between devices, extended_2(): lax.ppermute(lax.slice_in_dim(block, block.shape[dim] - width, None, axis...  39.3 us
    another operation x7, other arithmetic, local(): factor = jnp.linalg.cholesky(system)  24.8 us
    another operation x4, other arithmetic, local(): lax.linalg.triangular_solve(factor, halfway, left_side=True, lower=True,...  20.9 us
  transfers between devices with their start and end apart: 8, of which 8 were waited for; matrix products, arithmetic and copies ran while one was open for 1% of the time, Pallas kernels for 0%

profile of v1, /device:TPU:8, one launch (start us, length us, event | category | flops | bytes accessed | tf_op | source)
XLA Modules:
  0.0 990.7 jit_solution(4874920588327979472)
XLA Ops:
  6.5 2.0 copy.44
  8.6 2.6 bitcast_add_fusion.4
  11.2 4.0 fusion.20
  15.1 1.7 all_to_all.12
  16.9 1.2 copy.19
  18.1 54.5 %all_to_all.16 = f32[32,32,512]{2,0,1:T(8,128)S(1)} all-to-all(f32[32,32,512]{2,0,1:T(8,128)S(1)} %copy.19), channel_id=1, replica_groups=mesh['grp'=16,'row'=32] {'row'}, dimensions={1} | all-to-all | bytes 4194304 | tf_op jit(solution)/shard_map/all_to_all | solution.py:87
  72.5 1.1 fusion.66
  73.6 14.2 %collective-permute-start = (f32[2,128,512]{2,1,0:T(8,128)}, f32[2,128,512]{2,1,0:T(8,128)S(1)}, u32[]{:S(2)}, u32[]{:S(2)}) collective-permute-start(f32[2,128,512]{2,1,0:T(8,128)} %bitcast.2), channel_id=1, source_target_pairs={{0,32},{32,64},{64,96},{96,128},{128,160},{160,192},{192,224},{224... | collective-permute-start | bytes 1572872 | tf_op jit(solution)/shard_map/ppermute | solution.py:18
  87.8 1.9 collective-permute-start.1
  89.8 20.8 %collective-permute-done = f32[2,128,512]{2,1,0:T(8,128)S(1)} collective-permute-done((f32[2,128,512]{2,1,0:T(8,128)}, f32[2,128,512]{2,1,0:T(8,128)S(1)}, u32[]{:S(2)}, u32[]{:S(2)}) %collective-permute-start) | collective-permute-done | bytes 524320 | tf_op jit(solution)/shard_map/ppermute | solution.py:18
  110.6 0.5 collective-permute-done.1
  111.1 0.6 select_maximum_fusion.2
  111.7 1.8 fusion.62
  113.6 3.8 collective-permute-start.2
  117.4 3.0 collective-permute-start.3
  120.5 18.5 %collective-permute-done.2 = f32[2,128,512]{2,1,0:T(8,128)S(1)} collective-permute-done((f32[2,128,512]{2,1,0:T(8,128)S(1)}, f32[2,128,512]{2,1,0:T(8,128)S(1)}, u32[]{:S(2)}, u32[]{:S(2)}) %collective-permute-start.2) | collective-permute-done | bytes 524320 | tf_op jit(solution)/shard_map/ppermute | solution.py:18
  139.0 2.5 collective-permute-done.3
  141.5 0.6 select_maximum_fusion
  142.1 2.9 fusion.30
  145.0 2.6 gather_fusion.1
  147.6 0.8 bitcast_select_fusion.1
  148.5 1.8 copy.20
  150.4 2.6 gather_fusion
  153.0 0.9 select_bitcast_fusion.1
  153.9 94.2 %all-gather.3.cloned.1.call-done = f32[16,128,512]{2,1,0:T(8,128)} async-done(((f32[1,128,512]{2,1,0:T(8,128)}), f32[16,128,512]{2,1,0:T(8,128)}) %all-gather.3.cloned.1.call-update) | async-done | bytes 4194320 | tf_op jit(solution)/shard_map/all_gather | solution.py:104
  248.1 2.6 reduce_sum.18
  250.7 0.1 copy.21
  250.8 0.7 gather_fusion.2
  251.5 0.7 select_bitcast_fusion.3
  252.2 0.2 all-gather.5.cloned.1.call-start
  252.5 283.2 %all-reduce.13.cloned.1.call-done = (f32[1024,128]{0,1:T(8,128)}, f32[128,128]{0,1:T(8,128)}) async-done(((f32[1024,128]{0,1:T(8,128)}, f32[128,128]{0,1:T(8,128)}), (f32[1024,128]{0,1:T(8,128)}, f32[128,128]{0,1:T(8,128)})) %all-reduce.13.cloned.1.call-update) | async-done | bytes 589840 | tf_op jit(solution)/shard_map/psum | solution.py:110
  535.7 1.0 copy.23
  536.7 0.9 fusion.55
  537.6 0.1 copy.25
  537.7 0.1 copy.26
  537.8 11.7 %cholesky.44 = f32[128,128]{1,0:T(8,128)S(1)} custom-call(f32[128,128]{1,0:T(8,128)S(1)} %copy.26), custom_call_target="Cholesky" | custom-call | tf_op jit(solution)/shard_map/jit(cholesky)/cholesky | solution.py:112
  549.6 0.6 compare_reduce_fusion.1
  550.2 0.6 fusion.41
  550.9 9.8 custom-call.11
  560.7 0.4 fusion.49
  561.1 0.4 fusion.51
  561.5 3.4 convolution_subtract_fusion.1
  564.9 0.8 gather_fusion.4
  565.7 0.8 bitcast_select_fusion
  566.5 0.3 all-reduce.11.cloned.1.call-start
  566.8 1.8 copy.27
  568.6 2.6 gather_fusion.3
  571.2 0.9 select_bitcast_fusion
  572.1 95.4 %all-gather.5.cloned.1.call-done = f32[16,128,512]{2,1,0:T(8,128)} async-done(((f32[1,128,512]{2,1,0:T(8,128)}), f32[16,128,512]{2,1,0:T(8,128)}) %all-gather.5.cloned.1.call-update) | async-done | bytes 4194320 | tf_op jit(solution)/shard_map/all_gather | solution.py:104
  667.6 2.6 reduce_sum.19
  670.2 0.1 copy.28
  670.3 0.7 gather_fusion.5
  671.1 0.6 select_bitcast_fusion.2
  671.8 0.1 copy.31
  671.9 283.4 %all-reduce.11.cloned.1.call-done = (f32[1024,128]{0,1:T(8,128)}, f32[128,128]{1,0:T(8,128)}) async-done(((f32[1024,128]{0,1:T(8,128)}, f32[128,128]{1,0:T(8,128)}), (f32[1024,128]{0,1:T(8,128)}, f32[128,128]{1,0:T(8,128)})) %all-reduce.11.cloned.1.call-update) | async-done | bytes 589840 | tf_op jit(solution)/shard_map/psum | solution.py:110
  955.3 1.0 copy.30
  956.3 0.9 fusion.48
  957.4 11.7 %cholesky.55 = f32[128,128]{1,0:T(8,128)S(1)} custom-call(f32[128,128]{1,0:T(8,128)S(1)} %fusion.47), custom_call_target="Cholesky" | custom-call | tf_op jit(solution)/shard_map/jit(cholesky)/cholesky | solution.py:112
  969.1 0.6 compare_reduce_fusion
  969.7 0.7 fusion.42
  970.4 9.8 custom-call.13
  980.2 0.4 fusion.43
  980.7 0.4 fusion.45
  981.0 3.2 convolution_subtract_fusion
  (39 shorter events, 0.7 us)
Async XLA Ops:
  6.5 241.5 %all-gather.3.cloned.1.call-start = ((), (), s32[]{:S(2)}) async-start(), calls=%async_computation.1 | async-start | bytes 4456448 | tf_op jit(solution)/shard_map/all_gather | solution.py:104
  6.5 2.0 copy-start.3
  6.5 2.0 copy-start.4
  73.6 37.0 %collective-permute-start = (f32[2,128,512]{2,1,0:T(8,128)}, f32[2,128,512]{2,1,0:T(8,128)S(1)}, u32[]{:S(2)}, u32[]{:S(2)}) collective-permute-start(f32[2,128,512]{2,1,0:T(8,128)} %bitcast.2), channel_id=1, source_target_pairs={{0,32},{32,64},{64,96},{96,128},{128,160},{160,192},{192,224},{224... | collective-permute-start | bytes 1572872 | tf_op jit(solution)/shard_map/ppermute | solution.py:18
  87.8 23.3 %collective-permute-start.1 = (f32[2,128,512]{2,1,0:T(8,128)}, f32[2,128,512]{2,1,0:T(8,128)S(1)}, u32[]{:S(2)}, u32[]{:S(2)}) collective-permute-start(f32[2,128,512]{2,1,0:T(8,128)} %bitcast.4), channel_id=1, source_target_pairs={{32,0},{64,32},{96,64},{128,96},{160,128},{192,160},{224,192},{256... | collective-permute-start | bytes 1572872 | tf_op jit(solution)/shard_map/ppermute | solution.py:21
  113.5 6.8 copy-start.5
  113.6 25.3 %collective-permute-start.2 = (f32[2,128,512]{2,1,0:T(8,128)S(1)}, f32[2,128,512]{2,1,0:T(8,128)S(1)}, u32[]{:S(2)}, u32[]{:S(2)}) collective-permute-start(f32[2,128,512]{2,1,0:T(8,128)S(1)} %get-tuple-element.17), channel_id=1, source_target_pairs={{0,32},{32,64},{64,96},{96,128},{128,160},{160,192},{192,224},{224... | collective-permute-start | bytes 1572872 | tf_op jit(solution)/shard_map/ppermute | solution.py:18
  117.4 24.1 %collective-permute-start.3 = (f32[2,128,512]{2,1,0:T(8,128)S(1)}, f32[2,128,512]{2,1,0:T(8,128)S(1)}, u32[]{:S(2)}, u32[]{:S(2)}) collective-permute-start(f32[2,128,512]{2,1,0:T(8,128)S(1)} %get-tuple-element.16), channel_id=1, source_target_pairs={{32,0},{64,32},{96,64},{128,96},{160,128},{192,160},{224,192},{256... | collective-permute-start | bytes 1572872 | tf_op jit(solution)/shard_map/ppermute | solution.py:21
  145.0 3.5 copy-start
  148.4 387.2 %all-reduce.13.cloned.1.call-start = ((), (), s32[]{:S(2)}) async-start(), calls=%async_computation.4 | async-start | bytes 1179648 | tf_op jit(solution)/shard_map/psum | solution.py:110
  153.9 98.6 %copy-start.6 = (f32[2,128]{1,0:T(2,128)S(1)}, f32[2,128]{1,0:T(2,128)}, u32[]{:S(2)}) copy-start(f32[2,128]{1,0:T(2,128)} %param.14) | copy-start | bytes 3076
  252.2 415.3 %all-gather.5.cloned.1.call-start = ((), (), s32[]{:S(2)}) async-start(), calls=%async_computation.2 | async-start | bytes 4456448 | tf_op jit(solution)/shard_map/all_gather | solution.py:104
  535.7 25.8 %copy-start.1 = (f32[1024,128]{0,1:T(8,128)S(1)}, f32[1024,128]{0,1:T(8,128)}, u32[]{:S(2)}) copy-start(f32[1024,128]{0,1:T(8,128)} %get-tuple-element.10) | copy-start | bytes 1572868
  566.5 388.8 %all-reduce.11.cloned.1.call-start = ((), (), s32[]{:S(2)}) async-start(), calls=%async_computation.3 | async-start | bytes 1179648 | tf_op jit(solution)/shard_map/psum | solution.py:110
  955.3 25.8 %copy-start.2 = (f32[1024,128]{0,1:T(8,128)S(1)}, f32[1024,128]{0,1:T(8,128)}, u32[]{:S(2)}) copy-start(f32[1024,128]{0,1:T(8,128)} %get-tuple-element.6) | copy-start | bytes 1572868
Sparse Core Ops, SparseCore 0:
  148.6 99.4 all-gather.2
  252.4 283.2 all-reduce.12
  566.6 100.8 all-gather.4
  671.9 283.3 all-reduce.10
